TPU v7x, 256 devices: a whole 4x4x8 slice. The times are simulated.
256 devices in a mesh: inp: 4 (over y_lo, core), tm: 64 (over z, y_hi, x).
Axes of the slice: x: 4, y: 4 (y_hi: 2, y_lo: 2; y = y_hi * 2 + y_lo), z: 8, core: 2. Of those that a mesh axis runs over, the one named last changes fastest.
Arguments:
- samples: bfloat16 [2, 2048, 262144], P(None, 'inp', 'tm'), may hold values from -6 to 6
- weights: bfloat16 [2, 2048, 256], P(None, 'inp'), may hold values from -0.09375 to 0.09375
- filter_taps: float32 [8, 1024], replicated, may hold values from -2 to 2
Outputs:
- spectrum: float32 [256, 256, 2, 1024], P('inp', 'tm')
All inputs are finite; a program needn't handle non-finite values.
Results may differ from a plain program's by a relative error of at most 0.012.
Values may be sent and summed in bfloat16 or wider, within the bound.
A program may use at most 64 MiB of HBM per device.

v0:
```python
import functools

import jax
import jax.numpy as jnp
import ml_dtypes
import numpy as np
from jax import lax
from jax.experimental import pallas as pl
from jax.experimental.pallas import tpu as pltpu
from jax.sharding import PartitionSpec as P

MESH = pl.DeviceIdType.MESH
LANES = 128
ROW_CHIPS = 4


def transform_table(channels):
    at = np.arange(channels, dtype=np.int64)
    angle = (at[:, None] * at[None, :] % channels) * (2.0 * np.pi / channels)
    cos = (np.cos(angle) / np.sqrt(channels)).reshape(-1, LANES, channels)
    sin = (np.sin(angle) / np.sqrt(channels)).reshape(-1, LANES, channels)
    return np.concatenate([cos, sin], axis=1).astype(ml_dtypes.bfloat16)


def kernel(
    steps,
    frames,
    x_hbm,
    w_hbm,
    taps,
    tab_hbm,
    out,
    xbuf,
    wbuf,
    steer,
    pbuf,
    rbuf,
    sbuf,
    ybuf,
    fbuf,
    pin,
    qin,
    ap,
    aq,
    bp,
    bq,
    tab,
    lhs,
    xsem,
    wsem,
    tsem,
    r1s,
    r1r,
    r2s,
    r2r,
    ps,
    pr,
    qs,
    qr,
    rps,
    rqs,
    aps,
    aqs,
    bps,
    bqs,
):
    i, t = lax.axis_index("inp"), lax.axis_index("tm")
    last = lax.axis_size("tm") - 1
    core = lax.rem(i, 2)
    lo = i // 2
    x = lax.rem(t, ROW_CHIPS)
    first_col, end_col = x == 0, x == ROW_CHIPS - 1
    has_prev, has_next = t > 0, t < last
    other_i = lo * 2 + (1 - core)
    pair_i = (1 - lo) * 2 + core
    sibling = {"inp": other_i, "tm": t}
    pair = {"inp": pair_i, "tm": t}
    nxt = {"inp": jnp.where(end_col, pair_i, i), "tm": jnp.where(has_next, t + 1, t)}
    prv = {"inp": jnp.where(first_col, pair_i, i), "tm": jnp.where(has_prev, t - 1, t)}
    depth = x_hbm.shape[1]
    channels = taps.shape[1]
    beams = fbuf.shape[1] // 2
    half = beams
    width = frames * LANES

    def load_x(c, f):
        return pltpu.make_async_copy(
            x_hbm.at[:, :, pl.ds(pl.multiple_of(f * channels + c * LANES, LANES), LANES)],
            xbuf.at[c, :, :, pl.ds(f * LANES, LANES)],
            xsem.at[c, f],
        )

    load_w = pltpu.make_async_copy(w_hbm, wbuf, wsem)
    load_t = pltpu.make_async_copy(tab_hbm, tab, tsem)
    load_w.start()
    for f in range(frames):
        load_x(0, f).start()

    barrier = pltpu.get_barrier_semaphore()
    pl.semaphore_signal(barrier, inc=1, device_id=sibling, device_id_type=MESH)
    pl.semaphore_signal(barrier, inc=1, device_id=pair, device_id_type=MESH)

    @pl.when(has_prev)
    def _():
        pl.semaphore_signal(barrier, inc=1, device_id=prv, device_id_type=MESH)

    def start_x(c, carry):
        for f in range(frames):
            load_x(c, f).start()
        return carry

    lax.fori_loop(1, steps, start_x, 0)
    load_t.start()
    load_w.wait()
    for block in range(4):
        to_core, to_lo = block // 2, block % 2
        first = (to_lo * 2 + to_core) * beams
        base = to_lo * 2 * beams
        re = wbuf[0, :, first : first + beams].astype(jnp.float32).T.astype(jnp.bfloat16)
        im = wbuf[1, :, first : first + beams].astype(jnp.float32).T.astype(jnp.bfloat16)
        steer[to_core, base : base + beams, :depth] = re
        steer[to_core, base : base + beams, depth:] = -im
        steer[to_core, base + beams : base + 2 * beams, :depth] = im
        steer[to_core, base + beams : base + 2 * beams, depth:] = re

    @pl.when(jnp.logical_not(has_prev))
    def _():
        pin[...] = jnp.zeros_like(pin)
        qin[...] = jnp.zeros_like(qin)

    pl.semaphore_wait(barrier, jnp.where(has_next, 3, 2))

    def remote(src, dst, send, recv, to):
        return pltpu.make_async_remote_copy(
            src_ref=src, dst_ref=dst, send_sem=send, recv_sem=recv, device_id=to, device_id_type=MESH
        )

    def to_sibling(c):
        return remote(pbuf.at[c, 1 - core], rbuf.at[c], r1s.at[c], r1r.at[c], sibling)

    def to_pair(c):
        return remote(sbuf.at[c], ybuf.at[c], r2s.at[c], r2r.at[c], pair)

    def part(ref, c, h):
        return ref.at[c, pl.ds(h * half, half)]

    def own_on(c, h):
        return remote(part(fbuf, c, h), part(pin, c, h), ps.at[c, h], pr.at[c, h], nxt)

    def own_up(c):
        return remote(part(fbuf, c, 0), ap.at[c], ps.at[c, 0], aps.at[c], nxt)

    def own_across(c):
        return remote(part(fbuf, c, 1), bp.at[c], ps.at[c, 1], bps.at[c], pair)

    def late(c, h):
        return pin.at[c, pl.ds(h * half, half), pl.ds(LANES, width - LANES)]

    def old_on(c, h):
        return remote(late(c, h), part(qin, c, h), qs.at[c, h], qr.at[c, h], nxt)

    def old_up(c):
        return remote(late(c, 0), aq.at[c], qs.at[c, 0], aqs.at[c], nxt)

    def old_across(c):
        return remote(late(c, 1), bq.at[c], qs.at[c, 1], bqs.at[c], pair)

    def own_relay_first(c):
        return remote(ap.at[c], part(pin, c, 0), rps.at[c], pr.at[c, 0], pair)

    def own_relay_end(c):
        return remote(bp.at[c], part(pin, c, 1), rps.at[c], pr.at[c, 1], nxt)

    def old_relay_first(c):
        return remote(aq.at[c], part(qin, c, 0), rqs.at[c], qr.at[c, 0], pair)

    def old_relay_end(c):
        return remote(bq.at[c], part(qin, c, 1), rqs.at[c], qr.at[c, 1], nxt)

    in_row = jnp.logical_and(has_next, jnp.logical_not(end_col))
    row_end = jnp.logical_and(has_next, end_col)
    row_start = jnp.logical_and(has_prev, first_col)

    def form(c):
        for f in range(frames):
            load_x(c, f).wait()
        xs = xbuf[c].reshape(2 * depth, width)
        pbuf[c, 1 - core] = jnp.dot(
            steer[1 - core], xs, preferred_element_type=jnp.float32
        ).astype(jnp.bfloat16).reshape(2, 2 * beams, width)
        to_sibling(c).start()
        pbuf[c, core] = jnp.dot(
            steer[core], xs, preferred_element_type=jnp.float32
        ).astype(jnp.bfloat16).reshape(2, 2 * beams, width)

    def gather_chip(c):
        to_sibling(c).wait_recv()
        total = pbuf[c, core, 1 - lo].astype(jnp.float32) + rbuf[c, 1 - lo].astype(jnp.float32)
        sbuf[c] = total.astype(jnp.bfloat16)
        to_pair(c).start()

    def gather_pair(c):
        to_pair(c).wait_recv()
        total = (
            pbuf[c, core, lo].astype(jnp.float32)
            + rbuf[c, lo].astype(jnp.float32)
            + ybuf[c].astype(jnp.float32)
        )
        fbuf[c] = total.astype(jnp.bfloat16)

        @pl.when(in_row)
        def _():
            own_on(c, 0).start()
            own_on(c, 1).start()

        @pl.when(row_end)
        def _():
            own_up(c).start()
            own_across(c).start()

    def relay_own(c):
        @pl.when(row_start)
        def _():
            own_up(c).wait_recv()
            own_relay_first(c).start()

        @pl.when(row_end)
        def _():
            own_across(c).wait_recv()
            own_relay_end(c).start()

    def pass_old(c):
        @pl.when(has_prev)
        def _():
            own_on(c, 0).wait_recv()
            own_on(c, 1).wait_recv()

        @pl.when(in_row)
        def _():
            old_on(c, 0).start()
            old_on(c, 1).start()

        @pl.when(row_end)
        def _():
            old_up(c).start()
            old_across(c).start()

    def relay_old(c):
        @pl.when(row_start)
        def _():
            old_up(c).wait_recv()
            old_relay_first(c).start()

        @pl.when(row_end)
        def _():
            old_across(c).wait_recv()
            old_relay_end(c).start()

    def finish(c):
        @pl.when(has_prev)
        def _():
            old_on(c, 0).wait_recv()
            old_on(c, 1).wait_recv()

        @pl.when(c == 0)
        def _():
            load_t.wait()

        weights = taps[:, pl.ds(pl.multiple_of(c * LANES, LANES), LANES)]
        count = weights.shape[0]
        for p in range(2):
            rows = slice(p * beams, (p + 1) * beams)
            window = []
            for f in range(frames - 1):
                window.append(qin[c, rows, f * LANES : (f + 1) * LANES].astype(jnp.float32))
            for f in range(frames):
                window.append(pin[c, rows, f * LANES : (f + 1) * LANES].astype(jnp.float32))
            for f in range(frames):
                window.append(fbuf[c, rows, f * LANES : (f + 1) * LANES].astype(jnp.float32))
            for j in range(frames):
                total = weights[0:1] * window[j]
                for k in range(1, count):
                    total = total + weights[k : k + 1] * window[j + k]
                at = slice(j * beams, (j + 1) * beams)
                below = slice((frames + j) * beams, (frames + j + 1) * beams)
                value = total.astype(jnp.bfloat16)
                lhs[at, p * LANES : (p + 1) * LANES] = value
                if p == 0:
                    lhs[below, LANES:] = -value
                else:
                    lhs[below, :LANES] = value
        pieces = out.shape[1] // 256
        for n in range(pieces):
            cols = slice(n * 256, (n + 1) * 256)
            piece = jnp.dot(lhs[...], tab[c, :, cols], preferred_element_type=jnp.float32)

            @pl.when(c == 0)
            def _():
                out[:, cols] = piece

            @pl.when(c > 0)
            def _():
                out[:, cols] += piece

    stages = [
        (0, form),
        (1, gather_chip),
        (2, gather_pair),
        (3, relay_own),
        (4, pass_old),
        (5, relay_old),
        (6, finish),
    ]

    def turn(k, carry):
        for lag, stage in stages:
            c = k - lag

            @pl.when(jnp.logical_and(c >= 0, c < steps))
            def _():
                stage(c)

        return carry

    lax.fori_loop(0, steps + stages[-1][0], turn, 0)

    def drain(c, carry):
        to_sibling(c).wait_send()
        to_pair(c).wait_send()

        @pl.when(has_next)
        def _():
            for h in range(2):
                own_on(c, h).wait_send()
                old_on(c, h).wait_send()

        @pl.when(jnp.logical_or(row_start, row_end))
        def _():
            own_relay_first(c).wait_send()
            old_relay_first(c).wait_send()

        return carry

    lax.fori_loop(0, steps, drain, 0)


def body(samples, weights, filter_taps):
    depth, span = samples.shape[1:]
    owned = weights.shape[2] // lax.axis_size("inp")
    channels = filter_taps.shape[1]
    frames = span // channels
    steps = channels // LANES
    width = frames * LANES
    table = jnp.asarray(transform_table(channels))
    half = jnp.bfloat16
    dma = pltpu.SemaphoreType.DMA
    rows = 2 * owned
    anywhere = pl.BlockSpec(memory_space=pl.ANY)
    inside = pl.BlockSpec(memory_space=pltpu.VMEM)
    spectrum = pl.pallas_call(
        functools.partial(kernel, steps, frames),
        out_shape=jax.ShapeDtypeStruct((2 * frames * owned, channels), jnp.float32),
        in_specs=[anywhere, anywhere, inside, anywhere],
        out_specs=inside,
        scratch_shapes=[
            pltpu.VMEM((steps, 2, depth, width), half),
            pltpu.VMEM(weights.shape, half),
            pltpu.VMEM((2, 2 * rows, 2 * depth), half),
            pltpu.VMEM((steps, 2, 2, rows, width), half),
            pltpu.VMEM((steps, 2, rows, width), half),
            pltpu.VMEM((steps, rows, width), half),
            pltpu.VMEM((steps, rows, width), half),
            pltpu.VMEM((steps, rows, width), half),
            pltpu.VMEM((steps, rows, width), half),
            pltpu.VMEM((steps, rows, width - LANES), half),
            pltpu.VMEM((steps, owned, width), half),
            pltpu.VMEM((steps, owned, width - LANES), half),
            pltpu.VMEM((steps, owned, width), half),
            pltpu.VMEM((steps, owned, width - LANES), half),
            pltpu.VMEM(table.shape, half),
            pltpu.VMEM((2 * frames * owned, 2 * LANES), half),
            dma((steps, frames)),
            dma,
            dma,
            dma((steps,)),
            dma((steps,)),
            dma((steps,)),
            dma((steps,)),
            dma((steps, 2)),
            dma((steps, 2)),
            dma((steps, 2)),
            dma((steps, 2)),
            dma((steps,)),
            dma((steps,)),
            dma((steps,)),
            dma((steps,)),
            dma((steps,)),
            dma((steps,)),
        ],
        compiler_params=pltpu.CompilerParams(
            collective_id=0, has_side_effects=True, vmem_limit_bytes=52 << 20
        ),
        name="beams",
    )(samples, weights, filter_taps, table)
    return spectrum.reshape(2, frames, owned, channels).transpose(2, 1, 0, 3)


def solution(mesh):
    return jax.shard_map(
        body,
        mesh=mesh,
        in_specs=(P(None, "inp", "tm"), P(None, "inp", None), P()),
        out_specs=P("inp", "tm", None, None),
        check_vma=False,
    )
```

profile of v0, /device:TPU:160, one launch (start us, length us, event | category | flops | bytes accessed | tf_op | source)
XLA Modules:
  0.0 71.3 jit_solution(8714289701260148703)
XLA Ops:
  0.0 0.0 copy-start
  0.0 1.0 %copy-done = bf16[2,512,256]{2,1,0:T(8,128)(2,1)S(1)} copy-done((bf16[2,512,256]{2,1,0:T(8,128)(2,1)S(1)}, bf16[2,512,256]{2,1,0:T(8,128)(2,1)}, u32[]{:S(2)}) %copy-start) | copy-done | bytes 524312
  1.0 0.0 copy-start.1
  1.0 0.8 %copy-done.1 = f32[8,1024]{1,0:T(8,128)S(1)} copy-done((f32[8,1024]{1,0:T(8,128)S(1)}, f32[8,1024]{1,0:T(8,128)}, u32[]{:S(2)}) %copy-start.1) | copy-done | bytes 32792
  1.8 64.9 %beams.1 = f32[512,1024]{1,0:T(8,128)} custom-call(bf16[2,512,4096]{2,1,0:T(8,128)(2,1)} %x_hbm.1, bf16[2,512,256]{2,1,0:T(8,128)(2,1)S(1)} %copy-done, f32[8,1024]{1,0:T(8,128)S(1)} %copy-done.1, bf16[8,256,1024]{2,1,0:T(8,128)(2,1)} %constant.2.clone.tab_hbm), custom_call_target="tpu_custom_call" | custom-call | tf_op jit(solution)/shard_map/beams/pallas_call | solution.py:360
  66.7 4.5 %copy.7 = f32[2,4,64,1024]{3,0,1,2:T(2,128)} copy(f32[2,4,64,1024]{3,2,1,0:T(8,128)} %bitcast.4) | data formatting | bytes 4194304 | tf_op jit(solution)/shard_map/reshape | solution.py:405
Async XLA Ops:
  0.0 1.0 %copy-start = (bf16[2,512,256]{2,1,0:T(8,128)(2,1)S(1)}, bf16[2,512,256]{2,1,0:T(8,128)(2,1)}, u32[]{:S(2)}) copy-start(bf16[2,512,256]{2,1,0:T(8,128)(2,1)} %w_hbm.1) | copy-start | bytes 1572868
  1.0 0.8 %copy-start.1 = (f32[8,1024]{1,0:T(8,128)S(1)}, f32[8,1024]{1,0:T(8,128)}, u32[]{:S(2)}) copy-start(f32[8,1024]{1,0:T(8,128)} %taps.1) | copy-start | bytes 98308
where the time goes:
time: 72.1 us; the launch traced here: 71.3 us
  Pallas kernels  64.9 us (90%)
  local copies, waits for them, and re-layouts  6.33 us (9%)
    pallas_call x1, Pallas kernels, body(): pl.pallas_call(functools.partial(kernel, steps, frames), out_shape=jax.Sh...  64.9 us
    reshape x1, local copies, waits for them, and re-layouts, body(): return spectrum.reshape(2, frames, owned, channels).transpose(2, 1, 0, 3)  4.53 us
    unnamed x4, local copies, waits for them, and re-layouts  1.8 us

commit v1 on v0

v1 whole, which is shorter than its diff:
```python
import functools

import jax
import jax.numpy as jnp
import ml_dtypes
import numpy as np
from jax import lax
from jax.experimental import pallas as pl
from jax.experimental.pallas import tpu as pltpu
from jax.sharding import PartitionSpec as P

MESH = pl.DeviceIdType.MESH
LANES = 128
ROW_CHIPS = 4
LEFT_FRAMES = 2


def transform_table(channels):
    at = np.arange(channels, dtype=np.int64)
    angle = (at[:, None] * at[None, :] % channels) * (2.0 * np.pi / channels)
    cos = (np.cos(angle) / np.sqrt(channels)).reshape(-1, LANES, channels)
    sin = (np.sin(angle) / np.sqrt(channels)).reshape(-1, LANES, channels)
    return np.concatenate([cos, sin], axis=1).astype(ml_dtypes.bfloat16)


def kernel(
    steps,
    frames,
    x_hbm,
    w_hbm,
    taps_hbm,
    tab_hbm,
    out,
    xbuf,
    wbuf,
    taps,
    tab,
    steer,
    pbuf,
    rbuf,
    sbuf,
    ybuf,
    fbuf,
    pin,
    qin,
    lbuf,
    cbuf,
    gbuf,
    gmid,
    base,
    lhs,
    xsem,
    wsem,
    ksem,
    tsem,
    r1s,
    r1r,
    r2s,
    r2r,
    ps,
    pr,
    qs,
    qr,
    ls,
    lr,
    ms,
    cs,
    cr,
    ds,
    gs,
    gr,
    hs,
):
    i, t = lax.axis_index("inp"), lax.axis_index("tm")
    row_count = lax.axis_size("tm") // ROW_CHIPS
    core = lax.rem(i, 2)
    lo = i // 2
    x = lax.rem(t, ROW_CHIPS)
    row = t // ROW_CHIPS
    row_prev, row_next = row > 0, row < row_count - 1
    other_i = lo * 2 + (1 - core)
    pair_i = (1 - lo) * 2 + core
    sibling = {"inp": other_i, "tm": t}
    pair = {"inp": pair_i, "tm": t}
    back, on = ROW_CHIPS - 1, ROW_CHIPS - 1

    def near(by):
        return {"inp": i, "tm": t + by}

    def cross(by):
        return {"inp": pair_i, "tm": t + by}

    at0, at1, at2, at3 = x == 0, x == 1, x == 2, x == 3
    inner = x < 3
    row_end = jnp.logical_and(at3, row_next)
    row_start = jnp.logical_and(at0, row_prev)
    lead = jnp.logical_and(at2, row_next)
    trail = jnp.logical_and(at2, row_prev)
    fed = jnp.logical_and(at1, row_prev)

    depth = x_hbm.shape[1]
    channels = taps.shape[1]
    count = taps.shape[0]
    beams = fbuf.shape[1] // 2
    half = beams
    width = frames * LANES
    by_left = lbuf.shape[2]

    def load_x(c, f):
        return pltpu.make_async_copy(
            x_hbm.at[:, :, pl.ds(pl.multiple_of(f * channels + c * LANES, LANES), LANES)],
            xbuf.at[c, :, :, pl.ds(f * LANES, LANES)],
            xsem.at[c, f],
        )

    load_w = pltpu.make_async_copy(w_hbm, wbuf, wsem)
    load_k = pltpu.make_async_copy(taps_hbm, taps, ksem)
    load_t = pltpu.make_async_copy(tab_hbm, tab, tsem)
    load_w.start()
    for f in range(frames):
        load_x(0, f).start()

    barrier = pltpu.get_barrier_semaphore()

    def greet(device):
        pl.semaphore_signal(barrier, inc=1, device_id=device, device_id_type=MESH)

    greet(sibling)
    greet(pair)

    @pl.when(at0)
    def _():
        greet(near(1))

    @pl.when(row_start)
    def _():
        greet(cross(-1))

    @pl.when(at1)
    def _():
        greet(near(-1))

    @pl.when(fed)
    def _():
        greet(cross(-back))
        greet(cross(1))

    @pl.when(at2)
    def _():
        greet(near(-1))
        greet(near(1))

    @pl.when(lead)
    def _():
        greet(cross(1))

    @pl.when(trail)
    def _():
        greet(cross(-back))

    @pl.when(at3)
    def _():
        greet(near(-1))
        greet(near(-back))

    def start_x(c, carry):
        for f in range(frames):
            load_x(c, f).start()
        return carry

    lax.fori_loop(1, steps, start_x, 0)
    load_k.start()
    load_t.start()
    load_w.wait()
    for block in range(4):
        to_core, to_lo = block // 2, block % 2
        first = (to_lo * 2 + to_core) * beams
        top = to_lo * 2 * beams
        re = wbuf[0, :, first : first + beams].astype(jnp.float32).T.astype(jnp.bfloat16)
        im = wbuf[1, :, first : first + beams].astype(jnp.float32).T.astype(jnp.bfloat16)
        steer[to_core, top : top + beams, :depth] = re
        steer[to_core, top : top + beams, depth:] = -im
        steer[to_core, top + beams : top + 2 * beams, :depth] = im
        steer[to_core, top + beams : top + 2 * beams, depth:] = re

    @pl.when(jnp.logical_not(row_prev))
    def _():
        @pl.when(at0)
        def _():
            pin[...] = jnp.zeros_like(pin)

        @pl.when(at1)
        def _():
            qin[...] = jnp.zeros_like(qin)

    one = jnp.int32(1)
    ahead = jnp.where(row_next, one, 0)
    behind = jnp.where(row_prev, one, 0)
    sends = jnp.where(x < 2, 2, jnp.where(at2, 1 + ahead + behind, 1 + 3 * ahead))
    pl.semaphore_wait(barrier, 2 + sends)

    def remote(src, dst, send, recv, to):
        return pltpu.make_async_remote_copy(
            src_ref=src, dst_ref=dst, send_sem=send, recv_sem=recv, device_id=to, device_id_type=MESH
        )

    def to_sibling(c):
        return remote(pbuf.at[c, 1 - core], rbuf.at[c], r1s.at[c], r1r.at[c], sibling)

    def to_pair(c):
        return remote(sbuf.at[c], ybuf.at[c], r2s.at[c], r2r.at[c], pair)

    def rows(ref, c, h):
        return ref.at[c, pl.ds(h * half, half)]

    def own_on(c):
        return remote(fbuf.at[c], pin.at[c], ps.at[c], pr.at[c, 0], near(1))

    def own_left(c):
        src = fbuf.at[c, :, pl.ds(LANES, by_left)]
        to = {"inp": i, "tm": jnp.where(at0, t + on, t - 1)}
        return remote(src, lbuf.at[c], ls.at[c], lr.at[c], to)

    def left_on(c):
        to = {"inp": i, "tm": jnp.where(at0, t + on, t - 1)}
        return remote(lbuf.at[c], qin.at[c, :, pl.ds(0, by_left)], ms.at[c], qr.at[c, 0], to)

    def old_on(c):
        keep = width - LANES - by_left
        src = pin.at[c, :, pl.ds(LANES + by_left, keep)]
        return remote(src, qin.at[c, :, pl.ds(by_left, keep)], qs.at[c], qr.at[c, 1], near(1))

    def row_old(c, h):
        src = fbuf.at[c, pl.ds(h * half, half), pl.ds(LANES, width - LANES)]
        to = cross(-1) if h == 0 else cross(on)
        return remote(src, cbuf.at[c, h], cs.at[c, h], cr.at[c, h], to)

    def row_old_on(c, h):
        to = cross(on) if h == 0 else cross(-1)
        return remote(cbuf.at[c, h], rows(qin, c, h), ds.at[c, h], qr.at[c, h], to)

    def ahead_up(c, h):
        to = cross(1) if h == 0 else pair
        return remote(rows(gbuf, c, h), gmid.at[c], gs.at[c, h], gr.at[c], to)

    def ahead_on(c):
        h = jnp.where(at0, 0, 1)
        to = {"inp": pair_i, "tm": jnp.where(at0, t, t + 1)}
        dst = pin.at[c, pl.ds(pl.multiple_of(h * half, half), half)]
        return remote(gmid.at[c], dst, hs.at[c], pr.at[c, h], to)

    def ahead_in(c, h):
        return remote(gmid.at[c], rows(pin, c, h), hs.at[c], pr.at[c, h], pair)

    def form(c):
        for f in range(frames):
            load_x(c, f).wait()
        xs = xbuf[c].reshape(2 * depth, width)
        pbuf[c, 1 - core] = jnp.dot(
            steer[1 - core], xs, preferred_element_type=jnp.float32
        ).astype(jnp.bfloat16).reshape(2, 2 * beams, width)
        to_sibling(c).start()
        pbuf[c, core] = jnp.dot(
            steer[core], xs, preferred_element_type=jnp.float32
        ).astype(jnp.bfloat16).reshape(2, 2 * beams, width)

    def gather_chip(c):
        to_sibling(c).wait_recv()
        total = pbuf[c, core, 1 - lo].astype(jnp.float32) + rbuf[c, 1 - lo].astype(jnp.float32)
        sbuf[c] = total.astype(jnp.bfloat16)
        to_pair(c).start()

    def gather_pair(c):
        to_pair(c).wait_recv()
        total = (
            pbuf[c, core, lo].astype(jnp.float32)
            + rbuf[c, lo].astype(jnp.float32)
            + ybuf[c].astype(jnp.float32)
        )
        fbuf[c] = total.astype(jnp.bfloat16)

        @pl.when(inner)
        def _():
            own_on(c).start()

        @pl.when(x < 2)
        def _():
            own_left(c).start()

        @pl.when(row_end)
        def _():
            row_old(c, 0).start()
            row_old(c, 1).start()

    def chunk_taps(c):
        return taps[:, pl.ds(pl.multiple_of(c * LANES, LANES), LANES)]

    def frame(ref, c, at, f):
        return ref[c, at, f * LANES : (f + 1) * LANES].astype(jnp.float32)

    def pass_on(c):
        @pl.when(x > 0)
        def _():
            own_on(c).wait_recv()

        @pl.when(jnp.logical_or(at1, at2))
        def _():
            old_on(c).start()

        @pl.when(row_end)
        def _():
            weights = chunk_taps(c)
            for h in range(2):
                at = slice(h * half, (h + 1) * half)
                window = [frame(pin, c, at, f) for f in range(1, frames)]
                window += [frame(fbuf, c, at, f) for f in range(frames)]
                for j in range(frames):
                    total = weights[0:1] * window[j]
                    for k in range(1, count - 1 - j):
                        total = total + weights[k : k + 1] * window[j + k]
                    gbuf[c, at, j * LANES : (j + 1) * LANES] = total.astype(jnp.bfloat16)
                ahead_up(c, h).start()

    def relay_old(c):
        @pl.when(lead)
        def _():
            row_old(c, 0).wait_recv()
            row_old_on(c, 0).start()

        @pl.when(trail)
        def _():
            row_old(c, 1).wait_recv()
            row_old_on(c, 1).start()

        @pl.when(jnp.logical_or(at0, at3))
        def _():
            own_left(c).wait_recv()
            left_on(c).start()

    def relay_ahead(c):
        @pl.when(jnp.logical_or(row_start, row_end))
        def _():
            ahead_up(c, 0).wait_recv()
            ahead_on(c).start()

    def finish(c):
        @pl.when(row_start)
        def _():
            ahead_in(c, 0).wait_recv()
            ahead_in(c, 1).wait_recv()

        @pl.when(fed)
        def _():
            row_old_on(c, 0).wait_recv()
            row_old_on(c, 1).wait_recv()

        @pl.when(x > 1)
        def _():
            left_on(c).wait_recv()
            old_on(c).wait_recv()

        @pl.when(c == 0)
        def _():
            load_t.wait()

        weights = chunk_taps(c)

        @pl.when(at0)
        def _():
            base[...] = pin[c].astype(jnp.float32)

        @pl.when(x > 0)
        def _():
            for p in range(2):
                at = slice(p * beams, (p + 1) * beams)
                window = [frame(qin, c, at, f) for f in range(frames - 1)]
                window += [frame(pin, c, at, f) for f in range(frames)]
                for j in range(frames):
                    total = weights[0:1] * window[j]
                    for k in range(1, count - 1 - j):
                        total = total + weights[k : k + 1] * window[j + k]
                    base[at, j * LANES : (j + 1) * LANES] = total

        for p in range(2):
            at = slice(p * beams, (p + 1) * beams)
            window = [frame(fbuf, c, at, f) for f in range(frames)]
            for j in range(frames):
                total = base[at, j * LANES : (j + 1) * LANES]
                for f in range(j + 1):
                    k = count - 1 - j + f
                    total = total + weights[k : k + 1] * window[f]
                above = slice(j * beams, (j + 1) * beams)
                below = slice((frames + j) * beams, (frames + j + 1) * beams)
                value = total.astype(jnp.bfloat16)
                lhs[above, p * LANES : (p + 1) * LANES] = value
                if p == 0:
                    lhs[below, LANES:] = -value
                else:
                    lhs[below, :LANES] = value
        for n in range(channels // 256):
            cols = slice(n * 256, (n + 1) * 256)
            piece = jnp.dot(lhs[...], tab[c, :, cols], preferred_element_type=jnp.float32)

            @pl.when(c == 0)
            def _():
                out[:, cols] = piece

            @pl.when(c > 0)
            def _():
                out[:, cols] += piece

    stages = [
        (0, form),
        (1, gather_chip),
        (2, gather_pair),
        (3, pass_on),
        (3, relay_old),
        (4, relay_ahead),
        (5, finish),
    ]
    load_k.wait()

    def turn(k, carry):
        for lag, stage in stages:
            c = k - lag

            @pl.when(jnp.logical_and(c >= 0, c < steps))
            def _():
                stage(c)

        return carry

    lax.fori_loop(0, steps + stages[-1][0], turn, 0)

    def drain(c, carry):
        to_sibling(c).wait_send()
        to_pair(c).wait_send()

        @pl.when(inner)
        def _():
            own_on(c).wait_send()

        @pl.when(x < 2)
        def _():
            own_left(c).wait_send()

        @pl.when(jnp.logical_or(at0, at3))
        def _():
            left_on(c).wait_send()

        @pl.when(jnp.logical_or(at1, at2))
        def _():
            old_on(c).wait_send()

        @pl.when(row_end)
        def _():
            for h in range(2):
                row_old(c, h).wait_send()
                ahead_up(c, h).wait_send()

        @pl.when(lead)
        def _():
            row_old_on(c, 0).wait_send()

        @pl.when(trail)
        def _():
            row_old_on(c, 1).wait_send()

        @pl.when(jnp.logical_or(row_start, row_end))
        def _():
            ahead_on(c).wait_send()

        return carry

    lax.fori_loop(0, steps, drain, 0)


def spread(rows, out, sem):
    owned, frames = out.shape[:2]
    copies = []
    for part in range(2):
        for f in range(frames):
            at = (part * frames + f) * owned
            copies.append(
                pltpu.make_async_copy(rows.at[pl.ds(at, owned)], out.at[:, f, part], sem.at[part, f])
            )
    for copy in copies:
        copy.start()
    for copy in copies:
        copy.wait()


def body(samples, weights, filter_taps):
    depth, span = samples.shape[1:]
    owned = weights.shape[2] // lax.axis_size("inp")
    channels = filter_taps.shape[1]
    frames = span // channels
    steps = channels // LANES
    width = frames * LANES
    old = width - LANES
    table = jnp.asarray(transform_table(channels))
    half = jnp.bfloat16
    dma = pltpu.SemaphoreType.DMA
    rows = 2 * owned
    anywhere = pl.BlockSpec(memory_space=pltpu.HBM)
    inside = pl.BlockSpec(memory_space=pltpu.VMEM)
    one, two = dma((steps,)), dma((steps, 2))
    lines = pl.pallas_call(
        functools.partial(kernel, steps, frames),
        out_shape=jax.ShapeDtypeStruct((2 * frames * owned, channels), jnp.float32),
        in_specs=[anywhere] * 4,
        out_specs=inside,
        scratch_shapes=[
            pltpu.VMEM((steps, 2, depth, width), half),
            pltpu.VMEM(weights.shape, half),
            pltpu.VMEM(filter_taps.shape, jnp.float32),
            pltpu.VMEM(table.shape, half),
            pltpu.VMEM((2, 2 * rows, 2 * depth), half),
            pltpu.VMEM((steps, 2, 2, rows, width), half),
            pltpu.VMEM((steps, 2, rows, width), half),
            pltpu.VMEM((steps, rows, width), half),
            pltpu.VMEM((steps, rows, width), half),
            pltpu.VMEM((steps, rows, width), half),
            pltpu.VMEM((steps, rows, width), half),
            pltpu.VMEM((steps, rows, old), half),
            pltpu.VMEM((steps, rows, LEFT_FRAMES * LANES), half),
            pltpu.VMEM((steps, 2, owned, old), half),
            pltpu.VMEM((steps, rows, width), half),
            pltpu.VMEM((steps, owned, width), half),
            pltpu.VMEM((rows, width), jnp.float32),
            pltpu.VMEM((2 * frames * owned, 2 * LANES), half),
            dma((steps, frames)),
            dma,
            dma,
            dma,
            one,
            one,
            one,
            one,
            one,
            two,
            one,
            two,
            one,
            one,
            one,
            two,
            two,
            two,
            two,
            one,
            one,
        ],
        compiler_params=pltpu.CompilerParams(
            collective_id=0, has_side_effects=True, vmem_limit_bytes=61 << 20
        ),
        name="beams",
    )(samples, weights, filter_taps, table)
    return pl.pallas_call(
        spread,
        out_shape=jax.ShapeDtypeStruct((owned, frames, 2, channels), jnp.float32),
        in_specs=[inside],
        out_specs=pl.BlockSpec(memory_space=pltpu.HBM),
        scratch_shapes=[dma((2, frames))],
        name="spread",
    )(lines)


def solution(mesh):
    return jax.shard_map(
        body,
        mesh=mesh,
        in_specs=(P(None, "inp", "tm"), P(None, "inp", None), P()),
        out_specs=P("inp", "tm", None, None),
        check_vma=False,
    )
```

time: 72.1 us -> 62.3 us (0.86)
  local copies, waits for them, and re-layouts: 6.33 us -> 0 us
  Pallas kernels: 64.9 us -> 61.8 us
    pallas_call x1, Pallas kernels: 64.9 us -> 58.9 us  [body(): pl.pallas_call(functools.partial(kernel, steps, frames), out_shape=jax.Sh...]
    reshape x1 -> x0, local copies, waits for them, and re-layouts: 4.53 us -> none  [body(): return spectrum.reshape(2, frames, owned, channels).transpose(2, 1, 0, 3)]
    pallas_call x0 -> x1, Pallas kernels: none -> 2.96 us  [body(): pl.pallas_call(spread, out_shape=jax.ShapeDtypeStruct((owned, frames, 2,...]
    unnamed x4 -> x0, local copies, waits for them, and re-layouts: 1.8 us -> none
where the time goes in v1:
time: 62.3 us; the launch traced here: 61.9 us
  Pallas kernels  61.8 us (99%)
    pallas_call x1, Pallas kernels, body(): pl.pallas_call(functools.partial(kernel, steps, frames), out_shape=jax.Sh...  58.9 us
    pallas_call x1, Pallas kernels, body(): pl.pallas_call(spread, out_shape=jax.ShapeDtypeStruct((owned, frames, 2,...  2.96 us

profile of v1, /device:TPU:160, one launch (start us, length us, event | category | flops | bytes accessed | tf_op | source)
XLA Modules:
  0.0 61.9 jit_solution(1965486275578882968)
XLA Ops:
  0.0 58.9 %beams.1.rows = f32[512,1024]{1,0:T(8,128)} custom-call(bf16[2,512,4096]{2,1,0:T(8,128)(2,1)} %x_hbm.1, bf16[2,512,256]{2,1,0:T(8,128)(2,1)} %w_hbm.1, f32[8,1024]{1,0:T(8,128)} %taps_hbm.1, bf16[8,256,1024]{2,1,0:T(8,128)(2,1)} %constant.2.clone.tab_hbm), custom_call_target="tpu_custom_call" | custom-call | tf_op jit(solution)/shard_map/beams/pallas_call | solution.py:508
  58.9 3.0 %spread.1 = f32[64,4,2,1024]{3,2,1,0:T(2,128)} custom-call(f32[512,1024]{1,0:T(8,128)} %beams.1.rows), custom_call_target="tpu_custom_call" | custom-call | tf_op jit(solution)/shard_map/spread/pallas_call | solution.py:559

commit v2 on v1

v2 whole, which is shorter than its diff:
```python
import functools

import jax
import jax.numpy as jnp
import ml_dtypes
import numpy as np
from jax import lax
from jax.experimental import pallas as pl
from jax.experimental.pallas import tpu as pltpu
from jax.sharding import PartitionSpec as P

MESH = pl.DeviceIdType.MESH
LANES = 128
ROW_CHIPS = 4
AHEAD = 2
RIGHT = 1
DRAIN_LAG = 14


def transform_table(channels):
    at = np.arange(channels, dtype=np.int64)
    angle = (at[:, None] * at[None, :] % channels) * (2.0 * np.pi / channels)
    cos = (np.cos(angle) / np.sqrt(channels)).reshape(-1, LANES, channels)
    sin = (np.sin(angle) / np.sqrt(channels)).reshape(-1, LANES, channels)
    return np.concatenate([cos, sin], axis=1).astype(ml_dtypes.bfloat16)


def kernel(
    steps,
    frames,
    x_hbm,
    w_hbm,
    taps_hbm,
    tab_hbm,
    out,
    xbuf,
    wbuf,
    taps,
    tab,
    steer,
    pbuf,
    rbuf,
    sbuf,
    ybuf,
    fbuf,
    pin,
    qin,
    lbuf,
    cbuf,
    gbuf,
    gmid,
    base,
    lhs,
    xsem,
    wsem,
    ksem,
    tsem,
    r1s,
    r1r,
    r2s,
    r2r,
    ps,
    pr,
    qs,
    qr,
    ls,
    lr,
    ms,
    cs,
    cr,
    ds,
    gs,
    gr,
    hs,
):
    i, t = lax.axis_index("inp"), lax.axis_index("tm")
    row_count = lax.axis_size("tm") // ROW_CHIPS
    core = lax.rem(i, 2)
    lo = i // 2
    x = lax.rem(t, ROW_CHIPS)
    row = t // ROW_CHIPS
    row_prev, row_next = row > 0, row < row_count - 1
    other_i = lo * 2 + (1 - core)
    pair_i = (1 - lo) * 2 + core
    sibling = {"inp": other_i, "tm": t}
    pair = {"inp": pair_i, "tm": t}
    back, on = ROW_CHIPS - 1, ROW_CHIPS - 1

    def near(by):
        return {"inp": i, "tm": t + by}

    def cross(by):
        return {"inp": pair_i, "tm": t + by}

    at0, at1, at2, at3 = x == 0, x == 1, x == 2, x == 3
    inner = x < 3
    row_end = jnp.logical_and(at3, row_next)
    row_start = jnp.logical_and(at0, row_prev)
    lead = jnp.logical_and(at2, row_next)
    trail = jnp.logical_and(at2, row_prev)
    fed = jnp.logical_and(at1, row_prev)

    depth = x_hbm.shape[1]
    channels = taps.shape[1]
    count = taps.shape[0]
    part_rows = fbuf.shape[1] // 2
    beams = 2 * part_rows
    width = frames * LANES

    def load_x(c, f):
        return pltpu.make_async_copy(
            x_hbm.at[:, :, pl.ds(pl.multiple_of(f * channels + c * LANES, LANES), LANES)],
            xbuf.at[c, :, :, pl.ds(f * LANES, LANES)],
            xsem.at[c, f],
        )

    load_w = pltpu.make_async_copy(w_hbm, wbuf, wsem)
    load_k = pltpu.make_async_copy(taps_hbm, taps, ksem)
    load_t = pltpu.make_async_copy(tab_hbm, tab, tsem)
    load_w.start()
    for f in range(frames):
        load_x(0, f).start()

    barrier = pltpu.get_barrier_semaphore()

    def greet(device):
        pl.semaphore_signal(barrier, inc=1, device_id=device, device_id_type=MESH)

    greet(sibling)
    greet(pair)

    @pl.when(at0)
    def _():
        greet(near(1))

    @pl.when(row_start)
    def _():
        greet(cross(-1))

    @pl.when(at1)
    def _():
        greet(near(-1))

    @pl.when(fed)
    def _():
        greet(cross(-back))
        greet(cross(1))

    @pl.when(at2)
    def _():
        greet(near(-1))
        greet(near(1))

    @pl.when(lead)
    def _():
        greet(cross(1))

    @pl.when(trail)
    def _():
        greet(cross(-back))

    @pl.when(at3)
    def _():
        greet(near(-1))
        greet(near(-back))

    def start_x(c, carry):
        for f in range(frames):
            load_x(c, f).start()
        return carry

    lax.fori_loop(1, AHEAD, start_x, 0)
    load_k.start()
    load_w.wait()
    real, imag = wbuf[0].T, wbuf[1].T
    for block in range(8):
        to_core, h, to_lo = block // 4, block // 2 % 2, block % 2
        first = (to_lo * 2 + to_core) * beams + h * part_rows
        top = (h * 2 + to_lo) * beams
        mid, end = top + part_rows, top + 2 * part_rows
        re, im = real[first : first + part_rows], imag[first : first + part_rows]
        steer[to_core, top:mid, :depth] = re
        steer[to_core, top:mid, depth:] = -im
        steer[to_core, mid:end, :depth] = im
        steer[to_core, mid:end, depth:] = re

    @pl.when(jnp.logical_not(row_prev))
    def _():
        @pl.when(at0)
        def _():
            pin[...] = jnp.zeros_like(pin)

        @pl.when(at1)
        def _():
            qin[...] = jnp.zeros_like(qin)

    one = jnp.int32(1)
    ahead = jnp.where(row_next, one, 0)
    behind = jnp.where(row_prev, one, 0)
    sends = jnp.where(x < 2, 2, jnp.where(at2, 1 + ahead + behind, 1 + 3 * ahead))
    pl.semaphore_wait(barrier, 2 + sends)

    def remote(src, dst, send, recv, to):
        return pltpu.make_async_remote_copy(
            src_ref=src, dst_ref=dst, send_sem=send, recv_sem=recv, device_id=to, device_id_type=MESH
        )

    def to_sibling(s):
        return remote(pbuf.at[s, 1 - core], rbuf.at[s], r1s.at[s], r1r.at[s], sibling)

    def to_pair(s):
        return remote(sbuf.at[s], ybuf.at[s], r2s.at[s], r2r.at[s], pair)

    def own_on(s):
        return remote(fbuf.at[s], pin.at[s], ps.at[s], pr.at[s], near(1))

    def old_on(s):
        src = pin.at[s, :, pl.ds(LANES, width - LANES)]
        return remote(src, qin.at[s], qs.at[s], qr.at[s], near(1))

    def own_old(s):
        return fbuf.at[s, :, pl.ds(LANES, width - LANES)]

    def left():
        return {"inp": i, "tm": jnp.where(at0, t + on, t - 1)}

    def own_left(s):
        return remote(own_old(s), lbuf.at[s], ls.at[s], lr.at[s], left())

    def left_on(s):
        return remote(lbuf.at[s], qin.at[s], ms.at[s], qr.at[s], left())

    def row_old(s, h):
        to = cross(-1) if h == 0 else cross(on)
        return remote(own_old(s), cbuf.at[s], cs.at[s], cr.at[s], to)

    def row_old_on(s, h):
        to = cross(on) if h == 0 else cross(-1)
        return remote(cbuf.at[s], qin.at[s], ds.at[s], qr.at[s], to)

    def ahead_up(s, h):
        to = cross(1) if h == 0 else pair
        return remote(gbuf.at[s], gmid.at[s], gs.at[s], gr.at[s], to)

    def ahead_on(s, h):
        to = pair if h == 0 else cross(1)
        return remote(gmid.at[s], pin.at[s], hs.at[s], pr.at[s], to)

    def goes_left(s):
        return lax.rem(s, 4) >= RIGHT

    def relays_old(h):
        return lead if h == 0 else trail

    def relays_ahead(h):
        return row_start if h == 0 else row_end

    def form(s, h):
        if h == 1:
            return
        c = s // 2

        @pl.when(c + AHEAD < steps)
        def _():
            start_x(c + AHEAD, 0)

        @pl.when(c == AHEAD)
        def _():
            load_t.start()

        for f in range(frames):
            load_x(c, f).wait()
        xs = xbuf[c].reshape(2 * depth, width)
        for to_core in (1 - core, core):
            value = jnp.dot(steer[to_core], xs, preferred_element_type=jnp.float32)
            value = value.astype(jnp.bfloat16).reshape(2, 2, beams, width)
            for g in range(2):
                pbuf[s + g, to_core] = value[g]
                if to_core is not core:
                    to_sibling(s + g).start()

    def gather_chip(s, h):
        to_sibling(s).wait_recv()
        total = pbuf[s, core, 1 - lo].astype(jnp.float32) + rbuf[s, 1 - lo].astype(jnp.float32)
        sbuf[s] = total.astype(jnp.bfloat16)
        to_pair(s).start()

    def gather_pair(s, h):
        to_pair(s).wait_recv()
        total = (
            pbuf[s, core, lo].astype(jnp.float32)
            + rbuf[s, lo].astype(jnp.float32)
            + ybuf[s].astype(jnp.float32)
        )
        fbuf[s] = total.astype(jnp.bfloat16)

        @pl.when(inner)
        def _():
            own_on(s).start()

        @pl.when(jnp.logical_and(x < 2, goes_left(s)))
        def _():
            own_left(s).start()

        @pl.when(row_end)
        def _():
            row_old(s, h).start()

    def chunk_taps(s):
        return taps[:, pl.ds(pl.multiple_of(s // 2 * LANES, LANES), LANES)]

    def frame(ref, s, at, f):
        return ref[s, at, f * LANES : (f + 1) * LANES].astype(jnp.float32)

    def pass_on(s, h):
        @pl.when(x > 0)
        def _():
            own_on(s).wait_recv()

        @pl.when(jnp.logical_and(jnp.logical_or(at1, at2), jnp.logical_not(goes_left(s))))
        def _():
            old_on(s).start()

        @pl.when(row_end)
        def _():
            weights = chunk_taps(s)
            at = slice(0, 2 * part_rows)
            window = [frame(pin, s, at, f) for f in range(1, frames)]
            window += [frame(fbuf, s, at, f) for f in range(frames)]
            for j in range(frames):
                total = weights[0:1] * window[j]
                for k in range(1, count - 1 - j):
                    total = total + weights[k : k + 1] * window[j + k]
                gbuf[s, at, j * LANES : (j + 1) * LANES] = total.astype(jnp.bfloat16)
            ahead_up(s, h).start()

    def relay_old(s, h):
        @pl.when(relays_old(h))
        def _():
            row_old(s, h).wait_recv()
            row_old_on(s, h).start()

        @pl.when(jnp.logical_and(jnp.logical_or(at0, at3), goes_left(s)))
        def _():
            own_left(s).wait_recv()
            left_on(s).start()

    def relay_ahead(s, h):
        @pl.when(relays_ahead(h))
        def _():
            ahead_up(s, h).wait_recv()
            ahead_on(s, h).start()

    def finish(s, h):
        @pl.when(row_start)
        def _():
            ahead_on(s, h).wait_recv()

        @pl.when(jnp.logical_or(fed, x > 1))
        def _():
            old_on(s).wait_recv()

        if h == 0:

            @pl.when(s == 0)
            def _():
                load_t.wait()

        weights = chunk_taps(s)

        @pl.when(at0)
        def _():
            base[...] = pin[s].astype(jnp.float32)

        @pl.when(x > 0)
        def _():
            at = slice(0, 2 * part_rows)
            window = [frame(qin, s, at, f) for f in range(frames - 1)]
            window += [frame(pin, s, at, f) for f in range(frames)]
            for j in range(frames):
                total = weights[0:1] * window[j]
                for k in range(1, count - 1 - j):
                    total = total + weights[k : k + 1] * window[j + k]
                base[at, j * LANES : (j + 1) * LANES] = total

        for p in range(2):
            at = slice(p * part_rows, (p + 1) * part_rows)
            window = [frame(fbuf, s, at, f) for f in range(frames)]
            for j in range(frames):
                total = base[at, j * LANES : (j + 1) * LANES]
                for f in range(j + 1):
                    k = count - 1 - j + f
                    total = total + weights[k : k + 1] * window[f]
                above = slice(j * part_rows, (j + 1) * part_rows)
                below = slice((frames + j) * part_rows, (frames + j + 1) * part_rows)
                value = total.astype(jnp.bfloat16)
                lhs[above, p * LANES : (p + 1) * LANES] = value
                if p == 0:
                    lhs[below, LANES:] = -value
                else:
                    lhs[below, :LANES] = value
        lines = slice(h * 2 * frames * part_rows, (h + 1) * 2 * frames * part_rows)
        for n in range(channels // 256):
            cols = slice(n * 256, (n + 1) * 256)
            piece = jnp.dot(lhs[...], tab[s // 2, :, cols], preferred_element_type=jnp.float32)

            @pl.when(s < 2)
            def _():
                out[lines, cols] = piece

            @pl.when(s >= 2)
            def _():
                out[lines, cols] += piece

    def drain(s, h):
        to_sibling(s).wait_send()
        to_pair(s).wait_send()

        @pl.when(inner)
        def _():
            own_on(s).wait_send()

        @pl.when(row_end)
        def _():
            row_old(s, h).wait_send()
            ahead_up(s, h).wait_send()

        @pl.when(relays_old(h))
        def _():
            row_old_on(s, h).wait_send()

        @pl.when(relays_ahead(h))
        def _():
            ahead_on(s, h).wait_send()

        @pl.when(jnp.logical_and(x < 2, goes_left(s)))
        def _():
            own_left(s).wait_send()

        @pl.when(jnp.logical_and(jnp.logical_or(at0, at3), goes_left(s)))
        def _():
            left_on(s).wait_send()

        @pl.when(jnp.logical_and(jnp.logical_or(at1, at2), jnp.logical_not(goes_left(s))))
        def _():
            old_on(s).wait_send()

    stages = [
        (0, form),
        (1, gather_chip),
        (3, gather_pair),
        (5, pass_on),
        (5, relay_old),
        (7, relay_ahead),
        (DRAIN_LAG, drain),
        (9, finish),
    ]
    load_k.wait()

    def turn(k, carry):
        for now in range(2):
            for lag, stage in stages:
                s = 2 * k + now - lag

                @pl.when(jnp.logical_and(s >= 0, s < 2 * steps))
                def _():
                    stage(s, (now - lag) % 2)

        return carry

    turns = steps + (stages[-1][0] + 1) // 2
    lax.fori_loop(0, turns, turn, 0)

    def settle(c, carry):
        for h in range(2):
            drain(2 * c + h, h)
        return carry

    lax.fori_loop((turns * 2 - DRAIN_LAG) // 2, steps, settle, 0)


def spread(rows, out, sem):
    owned, frames = out.shape[:2]
    half = owned // 2
    copies = []
    for h in range(2):
        for part in range(2):
            for f in range(frames):
                at = ((h * 2 + part) * frames + f) * half
                to = out.at[pl.ds(h * half, half), f, part]
                copies.append(
                    pltpu.make_async_copy(rows.at[pl.ds(at, half)], to, sem.at[h, part, f])
                )
    for copy in copies:
        copy.start()
    for copy in copies:
        copy.wait()


def body(samples, weights, filter_taps):
    depth, span = samples.shape[1:]
    owned = weights.shape[2] // lax.axis_size("inp")
    channels = filter_taps.shape[1]
    frames = span // channels
    steps = channels // LANES
    width = frames * LANES
    old = width - LANES
    table = jnp.asarray(transform_table(channels))
    half = jnp.bfloat16
    dma = pltpu.SemaphoreType.DMA
    rows = 2 * owned
    units = 2 * steps
    anywhere = pl.BlockSpec(memory_space=pltpu.HBM)
    inside = pl.BlockSpec(memory_space=pltpu.VMEM)
    lines = pl.pallas_call(
        functools.partial(kernel, steps, frames),
        out_shape=jax.ShapeDtypeStruct((2 * frames * owned, channels), jnp.float32),
        in_specs=[anywhere] * 4,
        out_specs=inside,
        scratch_shapes=[
            pltpu.VMEM((steps, 2, depth, width), half),
            pltpu.VMEM(weights.shape, half),
            pltpu.VMEM(filter_taps.shape, jnp.float32),
            pltpu.VMEM(table.shape, half),
            pltpu.VMEM((2, 2 * rows, 2 * depth), half),
            pltpu.VMEM((units, 2, 2, owned, width), half),
            pltpu.VMEM((units, 2, owned, width), half),
            pltpu.VMEM((units, owned, width), half),
            pltpu.VMEM((units, owned, width), half),
            pltpu.VMEM((units, owned, width), half),
            pltpu.VMEM((units, owned, width), half),
            pltpu.VMEM((units, owned, old), half),
            pltpu.VMEM((units, owned, old), half),
            pltpu.VMEM((units, owned, old), half),
            pltpu.VMEM((units, owned, width), half),
            pltpu.VMEM((units, owned, width), half),
            pltpu.VMEM((owned, width), jnp.float32),
            pltpu.VMEM((frames * owned, 2 * LANES), half),
            dma((steps, frames)),
            dma,
            dma,
            dma,
            dma((units,)),
            dma((units,)),
            dma((units,)),
            dma((units,)),
            dma((units,)),
            dma((units,)),
            dma((units,)),
            dma((units,)),
            dma((units,)),
            dma((units,)),
            dma((units,)),
            dma((units,)),
            dma((units,)),
            dma((units,)),
            dma((units,)),
            dma((units,)),
            dma((units,)),
        ],
        compiler_params=pltpu.CompilerParams(
            collective_id=0, has_side_effects=True, vmem_limit_bytes=61 << 20
        ),
        name="beams",
    )(samples, weights, filter_taps, table)
    return pl.pallas_call(
        spread,
        out_shape=jax.ShapeDtypeStruct((owned, frames, 2, channels), jnp.float32),
        in_specs=[inside],
        out_specs=pl.BlockSpec(memory_space=pltpu.HBM),
        scratch_shapes=[dma((2, 2, frames))],
        name="spread",
    )(lines)


def solution(mesh):
    return jax.shard_map(
        body,
        mesh=mesh,
        in_specs=(P(None, "inp", "tm"), P(None, "inp", None), P()),
        out_specs=P("inp", "tm", None, None),
        check_vma=False,
    )
```

time: 62.3 us -> 60.3 us (0.968)
  Pallas kernels: 61.8 us -> 60.2 us
    pallas_call x1, Pallas kernels: 58.9 us -> 57.2 us  [body(): pl.pallas_call(functools.partial(kernel, steps, frames), out_shape=jax.Sh...]
where the time goes in v2:
time: 60.3 us; the launch traced here: 60.2 us
  Pallas kernels  60.2 us (100%)
    pallas_call x1, Pallas kernels, body(): pl.pallas_call(functools.partial(kernel, steps, frames), out_shape=jax.Sh...  57.2 us
    pallas_call x1, Pallas kernels, body(): pl.pallas_call(spread, out_shape=jax.ShapeDtypeStruct((owned, frames, 2,...  3.03 us

profile of v2, /device:TPU:160, one launch (start us, length us, event | category | flops | bytes accessed | tf_op | source)
XLA Modules:
  0.0 60.2 jit_solution(5944696127856128051)
XLA Ops:
  0.0 57.2 %beams.1.rows = f32[512,1024]{1,0:T(8,128)} custom-call(bf16[2,512,4096]{2,1,0:T(8,128)(2,1)} %x_hbm.1, bf16[2,512,256]{2,1,0:T(8,128)(2,1)} %w_hbm.1, f32[8,1024]{1,0:T(8,128)} %taps_hbm.1, bf16[8,256,1024]{2,1,0:T(8,128)(2,1)} %constant.2.clone.tab_hbm), custom_call_target="tpu_custom_call" | custom-call | tf_op jit(solution)/shard_map/beams/pallas_call | solution.py:515
  57.2 3.0 %spread.1 = f32[64,4,2,1024]{3,2,1,0:T(2,128)} custom-call(f32[512,1024]{1,0:T(8,128)} %beams.1.rows), custom_call_target="tpu_custom_call" | custom-call | tf_op jit(solution)/shard_map/spread/pallas_call | solution.py:566

commit v3 on v2

--- a/solution.py
+++ b/solution.py
@@ -194,6 +194,18 @@
         def _():
             qin[...] = jnp.zeros_like(qin)
 
+    def multiply(c, to_core):
+        xs = xbuf[c].reshape(2 * depth, width)
+        value = jnp.dot(steer[to_core], xs, preferred_element_type=jnp.float32)
+        value = value.astype(jnp.bfloat16).reshape(2, 2, beams, width)
+        pbuf[2 * c, to_core] = value[0]
+        pbuf[2 * c + 1, to_core] = value[1]
+
+    for f in range(frames):
+        load_x(0, f).wait()
+    multiply(0, 1 - core)
+    multiply(0, core)
+
     one = jnp.int32(1)
     ahead = jnp.where(row_next, one, 0)
     behind = jnp.where(row_prev, one, 0)
@@ -268,16 +280,18 @@
         def _():
             load_t.start()
 
-        for f in range(frames):
-            load_x(c, f).wait()
-        xs = xbuf[c].reshape(2 * depth, width)
-        for to_core in (1 - core, core):
-            value = jnp.dot(steer[to_core], xs, preferred_element_type=jnp.float32)
-            value = value.astype(jnp.bfloat16).reshape(2, 2, beams, width)
-            for g in range(2):
-                pbuf[s + g, to_core] = value[g]
-                if to_core is not core:
-                    to_sibling(s + g).start()
+        @pl.when(c > 0)
+        def _():
+            for f in range(frames):
+                load_x(c, f).wait()
+            multiply(c, 1 - core)
+
+        to_sibling(s).start()
+        to_sibling(s + 1).start()
+
+        @pl.when(c > 0)
+        def _():
+            multiply(c, core)
 
     def gather_chip(s, h):
         to_sibling(s).wait_recv()
@@ -450,7 +464,7 @@
         (1, gather_chip),
         (3, gather_pair),
         (5, pass_on),
-        (5, relay_old),
+        (6, relay_old),
         (7, relay_ahead),
         (DRAIN_LAG, drain),
         (9, finish),

time: 60.3 us -> 59.6 us (0.988)
  Pallas kernels: 60.2 us -> 59 us
    pallas_call x1, Pallas kernels: 57.2 us -> 56 us  [body(): pl.pallas_call(functools.partial(kernel, steps, frames), out_shape=jax.Sh...]
where the time goes in v3:
time: 59.6 us; the launch traced here: 59 us
  Pallas kernels  59 us (99%)
    pallas_call x1, Pallas kernels, body(): pl.pallas_call(functools.partial(kernel, steps, frames), out_shape=jax.Sh...  56 us
    pallas_call x1, Pallas kernels, body(): pl.pallas_call(spread, out_shape=jax.ShapeDtypeStruct((owned, frames, 2,...  3.03 us

profile of v3, /device:TPU:160, one launch (start us, length us, event | category | flops | bytes accessed | tf_op | source)
XLA Modules:
  0.0 59.0 jit_solution(6888080143128869899)
XLA Ops:
  0.0 56.0 %beams.1.rows = f32[512,1024]{1,0:T(8,128)} custom-call(bf16[2,512,4096]{2,1,0:T(8,128)(2,1)} %x_hbm.1, bf16[2,512,256]{2,1,0:T(8,128)(2,1)} %w_hbm.1, f32[8,1024]{1,0:T(8,128)} %taps_hbm.1, bf16[8,256,1024]{2,1,0:T(8,128)(2,1)} %constant.2.clone.tab_hbm), custom_call_target="tpu_custom_call" | custom-call | tf_op jit(solution)/shard_map/beams/pallas_call | solution.py:529
  56.0 3.0 %spread.1 = f32[64,4,2,1024]{3,2,1,0:T(2,128)} custom-call(f32[512,1024]{1,0:T(8,128)} %beams.1.rows), custom_call_target="tpu_custom_call" | custom-call | tf_op jit(solution)/shard_map/spread/pallas_call | solution.py:580

commit v4 on v3

--- a/solution.py
+++ b/solution.py
@@ -259,7 +259,7 @@
         return remote(gmid.at[s], pin.at[s], hs.at[s], pr.at[s], to)
 
     def goes_left(s):
-        return lax.rem(s, 4) >= RIGHT
+        return lax.rem(s, 3) >= RIGHT
 
     def relays_old(h):
         return lead if h == 0 else trail

time: 59.6 us -> 59.9 us (level)
  Pallas kernels: 59 us -> 59.7 us
    pallas_call x1, Pallas kernels: 56 us -> 56.6 us  [body(): pl.pallas_call(functools.partial(kernel, steps, frames), out_shape=jax.Sh...]
where the time goes in v4:
time: 59.9 us; the launch traced here: 59.7 us
  Pallas kernels  59.7 us (100%)
    pallas_call x1, Pallas kernels, body(): pl.pallas_call(functools.partial(kernel, steps, frames), out_shape=jax.Sh...  56.6 us
    pallas_call x1, Pallas kernels, body(): pl.pallas_call(spread, out_shape=jax.ShapeDtypeStruct((owned, frames, 2,...  3.03 us

profile of v4, /device:TPU:160, one launch (start us, length us, event | category | flops | bytes accessed | tf_op | source)
XLA Modules:
  0.0 59.7 jit_solution(5473121097957005010)
XLA Ops:
  0.0 56.6 %beams.1.rows = f32[512,1024]{1,0:T(8,128)} custom-call(bf16[2,512,4096]{2,1,0:T(8,128)(2,1)} %x_hbm.1, bf16[2,512,256]{2,1,0:T(8,128)(2,1)} %w_hbm.1, f32[8,1024]{1,0:T(8,128)} %taps_hbm.1, bf16[8,256,1024]{2,1,0:T(8,128)(2,1)} %constant.2.clone.tab_hbm), custom_call_target="tpu_custom_call" | custom-call | tf_op jit(solution)/shard_map/beams/pallas_call | solution.py:529
  56.6 3.0 %spread.1 = f32[64,4,2,1024]{3,2,1,0:T(2,128)} custom-call(f32[512,1024]{1,0:T(8,128)} %beams.1.rows), custom_call_target="tpu_custom_call" | custom-call | tf_op jit(solution)/shard_map/spread/pallas_call | solution.py:580
